TPU v7x, 128 devices: a whole 4x4x4 slice. The times are simulated.
128 devices in a mesh: slab: 8 (over z, core), space: 16 (over y, x).
Axes of the slice: x: 4, y: 4, z: 4, core: 2. Of those that a mesh axis runs over, the one named last changes fastest.
Arguments:
- frames: bfloat16 [128, 128, 128, 128], P('slab', 'space'), may hold values from -6 to 6
- frame_dest: int32 [128], replicated, may hold values from 0 to 127, as said below
- clip_lengths: int32 [8], replicated, may hold values from 1 to 32, 128 in all
- norm_gain: float32 [128], replicated, may hold values from 0.5 to 1.5
- conv_bias: float32 [128], replicated, may hold values from -3 to 3
- conv_weight: bfloat16 [3, 3, 3, 128, 128], replicated, may hold values from -0.109375 to 0.109375
Outputs:
- encoded: float32 [128, 128, 128, 128], P('slab', None, 'space')
Inputs may be any that keep to these rules, and one draw needn't show every extreme that they name: frame_dest is a permutation; for every two slab indices a and b exactly 2 of the frames a * 16 to a * 16 + 15 go to positions b * 16 to b * 16 + 15.
All inputs are finite; a program needn't handle non-finite values.
Results may differ from a plain program's by a relative error of at most 0.0014.
Values may be sent and summed in bfloat16 or wider, within the bound.
A program may use at most 128 MiB of HBM per device.

v0:
```python
import jax
import jax.numpy as jnp
from jax import lax
from jax.sharding import PartitionSpec as P


def passed_along(block, axis, distance):
    devices = range(lax.axis_size(axis))
    route = [(i - distance, i) for i in devices if i - distance in devices]
    return lax.ppermute(block, axis, route)


def with_halo(block, sides, width):
    for axis, dim in sides:
        count = lax.axis_size(axis)
        forward = [(i, i + 1) for i in range(count - 1)]
        backward = [(target, source) for source, target in forward]
        low = lax.ppermute(
            lax.slice_in_dim(block, block.shape[dim] - width, None, axis=dim), axis, forward
        )
        high = lax.ppermute(lax.slice_in_dim(block, 0, width, axis=dim), axis, backward)
        block = jnp.concatenate([low, block, high], axis=dim)
    return block


def clip_masks(clip_lengths, positions):
    starts = jnp.cumsum(clip_lengths) - clip_lengths
    first_frame = jnp.max(
        jnp.where(starts[None, :] <= positions[:, None], starts[None, :], 0), axis=1
    )
    lags = jnp.arange(3, dtype=jnp.int32)
    return (positions[:, None] - lags[None, :] >= first_frame[:, None]).astype(jnp.bfloat16)


def normalize(arranged, norm_gain):
    values = arranged.astype(jnp.float32)
    meansq = jnp.mean(values * values, axis=-1, keepdims=True)
    return jax.nn.silu(values * lax.rsqrt(meansq + 1e-06) * norm_gain).astype(jnp.bfloat16)


def spatial_conv(inputs, kernel, padding):
    return lax.conv_general_dilated(
        inputs,
        kernel,
        (1, 1),
        padding,
        dimension_numbers=("NHWC", "HWIO", "NHWC"),
        preferred_element_type=jnp.float32,
    )


def with_earlier(normed):
    count = normed.shape[0]
    earlier = passed_along(normed[count - 2 :], "slab", 1)
    return jnp.concatenate([earlier, normed], axis=0)


def causal_branch(padded, masks, conv_weight, conv_bias, padding):
    count = masks.shape[0]
    branch = None
    for frame_lag in range(3):
        taps_in = (
            padded[2 - frame_lag : 2 - frame_lag + count] * masks[:, frame_lag][:, None, None, None]
        )
        term = spatial_conv(taps_in, conv_weight[frame_lag], padding)
        branch = term if branch is None else branch + term
    return branch + conv_bias


def local(frames, frame_dest, clip_lengths, norm_gain, conv_bias, conv_weight):
    slab_count = lax.axis_size("slab")
    slab_frames = frames.shape[0]
    per_peer = slab_frames // slab_count
    slab_pos = lax.axis_index("slab")
    own_dest = lax.dynamic_slice_in_dim(frame_dest, slab_pos * slab_frames, slab_frames)
    ordering = jnp.argsort(own_dest)
    packed = jnp.take(frames, ordering, axis=0)
    positions = slab_pos * slab_frames + jnp.arange(slab_frames, dtype=jnp.int32)
    inverse = jnp.argsort(frame_dest)
    sources = jnp.take(inverse, positions)
    source_slab = sources // slab_frames
    dest_table = jnp.take(frame_dest.reshape(slab_count, slab_frames), source_slab, axis=0)
    arrival = jnp.sum(
        ((dest_table >= slab_pos * slab_frames) & (dest_table < positions[:, None])).astype(
            jnp.int32
        ),
        axis=1,
    )
    picks = source_slab * per_peer + arrival
    masks = clip_masks(clip_lengths, positions)
    received = lax.all_to_all(packed, "slab", split_axis=0, concat_axis=0, tiled=True)
    arranged = jnp.take(received, picks, axis=0)
    normed = normalize(arranged, norm_gain)
    extended = with_earlier(normed)
    padded = with_halo(extended, (("space", 1),), 1)
    branch = causal_branch(padded, masks, conv_weight, conv_bias, ((0, 0), (1, 1)))
    encoded = arranged.astype(jnp.float32) + branch
    return lax.all_to_all(encoded, "space", split_axis=2, concat_axis=1, tiled=True)


def solution(mesh):
    placed = (P("slab", "space", None, None), P(), P(), P(), P(), P())
    return jax.shard_map(
        local, mesh=mesh, in_specs=placed, out_specs=P("slab", None, "space", None), check_vma=False
    )
```

profile of v0, /device:TPU:64, one launch (start us, length us, event | category | flops | bytes accessed | tf_op | source)
XLA Modules:
  0.0 284.4 jit_solution(7487285228178824776)
XLA Ops:
  0.0 0.7 dynamic_slice.3
  0.7 1.2 sort.34
  2.0 5.3 %gather_fusion.2 = bf16[16,8,128,128]{3,2,1,0:T(8,128)(2,1)} fusion(bf16[16,8,128,128]{3,2,1,0:T(8,128)(2,1)} %param.8, s32[1024]{0:T(1024)S(1)} %pad_clamp_fusion.1), kind=kCustom, calls=%fused_computation.clone | custom fusion | bytes 8388672 | tf_op jit(solution)/shard_map/jit(_take)/gather | solution.py:77
  7.3 4.7 %broadcast_select_fusion = bf16[16,8,128,128]{3,2,1,0:T(8,128)(2,1)} fusion(bf16[16,8,128,128]{3,2,1,0:T(8,128)(2,1)} %gather_fusion.2, pred[16]{0:T(512)(128)(4,1)S(1)} %compare_and_fusion.1), kind=kLoop, calls=%fused_computation.23 | loop fusion | flops 2097152 | bytes 8388624 | tf_op jit(solution)/shard_map/jit(_take)/select_n | solution.py:77
  12.0 5.0 %all-to-all-start = ((bf16[16,8,128,128]{3,2,1,0:T(8,128)(2,1)}), bf16[16,8,128,128]{3,2,1,0:T(8,128)(2,1)}, u32[]{:S(2)}, u32[]{:S(2)}) async-start(bf16[16,8,128,128]{3,2,1,0:T(8,128)(2,1)} %broadcast_select_fusion), calls=%async_computation | async-start | bytes 8388608 | tf_op jit(solution)/shard_map/all_to_all | solution.py:91
  17.0 2.5 sort.35
  19.6 0.7 gather_fusion
  20.3 0.6 gather_fusion.1
  20.9 0.2 convert_reduce_fusion
  21.1 42.5 %all-to-all-done = bf16[16,8,128,128]{3,2,1,0:T(8,128)(2,1)} async-done(((bf16[16,8,128,128]{3,2,1,0:T(8,128)(2,1)}), bf16[16,8,128,128]{3,2,1,0:T(8,128)(2,1)}, u32[]{:S(2)}, u32[]{:S(2)}) %all-to-all-start) | async-done | bytes 4194336 | tf_op jit(solution)/shard_map/all_to_all | solution.py:91
  63.6 5.2 %gather_fusion.3 = bf16[16,8,128,128]{3,2,1,0:T(8,128)(2,1)} fusion(bf16[16,8,128,128]{3,2,1,0:T(8,128)(2,1)} %all-to-all-done, s32[1024]{0:T(1024)S(1)} %pad_clamp_fusion), kind=kCustom, calls=%fused_computation.1.clone | custom fusion | bytes 8388672 | tf_op jit(solution)/shard_map/jit(_take)/gather | solution.py:92
  68.8 4.9 %fusion = f32[16,8,128]{0,2,1:T(8,128)S(1)} fusion(bf16[16,8,128,128]{3,2,1,0:T(8,128)(2,1)} %gather_fusion.3, pred[16]{0:T(512)(128)(4,1)S(1)} %get-tuple-element.10), kind=kLoop, calls=%fused_computation.7 | loop fusion | flops 8372224 | bytes 4259856 | tf_op jit(solution)/shard_map/reduce_sum | solution.py:37
  73.9 0.2 copy.34
  74.1 7.2 %fusion.7 = bf16[16,8,128,128]{3,0,2,1:T(8,128)(2,1)S(1)} fusion(f32[128]{0:T(128)S(1)} %copy-done.3, f32[16,8,128]{0,2,1:T(8,128)S(1)} %copy.34, bf16[16,8,128,128]{3,2,1,0:T(8,128)(2,1)} %gather_fusion.3, pred[16]{0:T(512)(128)(4,1)S(1)} %get-tuple-element.10), kind=kLoop, calls=%fused_computation.14 | loop fusion | flops 18874368 | bytes 8454672 | tf_op jit(solution)/shard_map/convert_element_type | solution.py:38
  81.3 2.0 copy-done
  83.3 0.5 slice.56
  83.9 1.9 collective-permute-start
  86.0 8.4 %collective-permute-done = bf16[2,8,128,128]{3,0,2,1:T(2,128)(2,1)S(1)} collective-permute-done((bf16[2,8,128,128]{3,0,2,1:T(2,128)(2,1)S(1)}, bf16[2,8,128,128]{3,0,2,1:T(2,128)(2,1)S(1)}, u32[]{:S(2)}, u32[]{:S(2)}) %collective-permute-start) | collective-permute-done | bytes 524320 | tf_op jit(solution)/shard_map/ppermute | solution.py:10
  94.4 1.9 pad_maximum_fusion.2
  96.5 1.3 collective-permute-start.2
  97.8 4.8 %collective-permute-start.1 = (bf16[18,1,128,128]{3,2,1,0:T(8,128)(2,1)S(1)}, bf16[18,1,128,128]{3,2,1,0:T(8,128)(2,1)S(1)}, u32[]{:S(2)}, u32[]{:S(2)}) collective-permute-start(bf16[18,1,128,128]{3,2,1,0:T(8,128)(2,1)S(1)} %copy.35), channel_id=1, source_target_pairs={{0,1},{1,2},{2,3},{3,4},{4,5},{5,6},{6,7},{7,8},{8,9},{9,10},{10,1... | collective-permute-start | bytes 1769480 | tf_op jit(solution)/shard_map/ppermute | solution.py:18
  102.7 10.8 %collective-permute-done.2 = bf16[18,1,128,128]{3,2,1,0:T(8,128)(2,1)S(1)} collective-permute-done((bf16[18,1,128,128]{3,2,1,0:T(8,128)(2,1)S(1)}, bf16[18,1,128,128]{3,2,1,0:T(8,128)(2,1)S(1)}, u32[]{:S(2)}, u32[]{:S(2)}) %collective-permute-start.2) | collective-permute-done | bytes 589856 | tf_op jit(solution)/shard_map/ppermute | solution.py:21
  113.5 0.4 copy.38
  113.9 0.8 collective-permute-done.1
  114.7 0.4 copy.37
  115.1 3.0 %pad_maximum_fusion = bf16[18,10,128,128]{3,0,2,1:T(8,128)(2,1)S(1)} fusion(bf16[18,1,128,128]{3,0,2,1:T(8,128)(2,1)S(1)} %copy.38, bf16[16,8,128,128]{3,0,2,1:T(8,128)(2,1)S(1)} %copy-done.1, bf16[2,8,128,128]{3,0,2,1:T(2,128)(2,1)S(1)} %collective-permute-done, bf16[18,1,128,128]{3,0,2,1:T(8,128)(2,1)S(1)} %copy.37), kind=kLoop, calls=%fused_computation.15 | loop fusion | flops 23592960 | bytes 11796480 | tf_op jit(solution)/shard_map/concatenate | solution.py:22
  118.2 12.3 %fusion.9 = f32[16,8,128,128]{3,0,2,1:T(8,128)} fusion(bf16[18,10,128,128]{3,0,2,1:T(8,128)(2,1)S(1)} %pad_maximum_fusion, bf16[16]{0:T(256)(128)(2,1)S(1)} %get-tuple-element.17, bf16[3,3,3,128,128]{4,3,2,1,0:T(8,128)(2,1)S(1)} %copy-done.5), kind=kOutput, calls=%fused_computation.19 | convolution fusion | flops 4817158144 | bytes 13926912 | tf_op jit(solution)/shard_map/conv_general_dilated | solution.py:42
  130.5 12.3 %fusion.10 = f32[16,8,128,128]{3,0,2,1:T(8,128)} fusion(bf16[18,10,128,128]{3,0,2,1:T(8,128)(2,1)S(1)} %pad_maximum_fusion, bf16[16]{0:T(256)(128)(2,1)S(1)} %get-tuple-element.18, bf16[3,3,3,128,128]{4,3,2,1,0:T(8,128)(2,1)S(1)} %copy-done.5), kind=kOutput, calls=%fused_computation.21 | convolution fusion | flops 4817158144 | bytes 13926912 | tf_op jit(solution)/shard_map/conv_general_dilated | solution.py:42
  142.8 23.1 %convert_add_fusion = f32[16,8,128,128]{3,0,2,1:T(8,128)} fusion(f32[16,8,128,128]{3,0,2,1:T(8,128)} %fusion.10, f32[16,8,128,128]{3,0,2,1:T(8,128)} %fusion.9, f32[128]{0:T(128)S(1)} %copy-done.7, bf16[18,10,128,128]{3,0,2,1:T(8,128)(2,1)S(1)} %pad_maximum_fusion, bf16[16]{0:T(256)(128)(2,1)S(1)} %get-tuple-element.16, ...), kind=kOutput, calls=%fused_computation.4 | convolution fusion | flops 4829741056 | bytes 34899456 | tf_op jit(solution)/shard_map/conv_general_dilated | solution.py:42
  165.8 4.4 %copy.39 = f32[16,8,128,128]{3,0,1,2:T(8,128)S(1)} copy(f32[16,8,128,128]{3,0,2,1:T(8,128)} %convert_add_fusion) | data formatting | bytes 16777216 | tf_op jit(solution)/shard_map/add | solution.py:97
  170.3 105.9 %all_to_all.23 = f32[16,8,128,128]{3,0,1,2:T(8,128)S(1)} all-to-all(f32[16,8,128,128]{3,0,1,2:T(8,128)S(1)} %copy.39), channel_id=1, replica_groups=mesh['slab'=8,'space'=16] {'space'}, dimensions={2} | all-to-all | bytes 16777216 | tf_op jit(solution)/shard_map/all_to_all | solution.py:98
  276.2 8.3 %copy.40 = f32[16,16,8,8,128]{4,3,2,1,0:T(8,128)} copy(f32[16,16,8,8,128]{4,0,2,3,1:T(8,128)S(1)} %bitcast.30) | data formatting | bytes 16777216 | tf_op jit(solution)/shard_map/all_to_all | solution.py:98
  (38 shorter events, 0.9 us)
Async XLA Ops:
  7.3 9.6 %copy-start.4 = (s32[128]{0:T(128)S(1)}, s32[128]{0:T(128)}, u32[]{:S(2)}) copy-start(s32[128]{0:T(128)} %param.9) | copy-start | bytes 1540
  12.0 51.6 %all-to-all-start = ((bf16[16,8,128,128]{3,2,1,0:T(8,128)(2,1)}), bf16[16,8,128,128]{3,2,1,0:T(8,128)(2,1)}, u32[]{:S(2)}, u32[]{:S(2)}) async-start(bf16[16,8,128,128]{3,2,1,0:T(8,128)(2,1)} %broadcast_select_fusion), calls=%async_computation | async-start | bytes 8388608 | tf_op jit(solution)/shard_map/all_to_all | solution.py:91
  16.9 57.2 %copy-start.3 = (f32[128]{0:T(128)S(1)}, f32[128]{0:T(128)}, u32[]{:S(2)}) copy-start(f32[128]{0:T(128)} %param.11) | copy-start | bytes 1540
  68.8 17.0 %copy-start.6 = (s32[8]{0:T(128)S(1)}, s32[8]{0:T(128)}, u32[]{:S(2)}) copy-start(s32[8]{0:T(128)} %param.10) | copy-start | bytes 100
  81.3 2.0 copy-start
  83.9 10.5 %collective-permute-start = (bf16[2,8,128,128]{3,0,2,1:T(2,128)(2,1)S(1)}, bf16[2,8,128,128]{3,0,2,1:T(2,128)(2,1)S(1)}, u32[]{:S(2)}, u32[]{:S(2)}) collective-permute-start(bf16[2,8,128,128]{3,0,2,1:T(2,128)(2,1)S(1)} %slice.56), channel_id=1, source_target_pairs={{0,16},{16,32},{32,48},{48,64},{64,80},{80,96},{96,112},{1,17},{17... | collective-permute-start | bytes 1572872 | tf_op jit(solution)/shard_map/ppermute | solution.py:10
  86.0 29.1 %copy-start.1 = (bf16[16,8,128,128]{3,0,2,1:T(8,128)(2,1)S(1)}, bf16[16,8,128,128]{3,0,2,1:T(8,128)(2,1)}, u32[]{:S(2)}) copy-start(bf16[16,8,128,128]{3,0,2,1:T(8,128)(2,1)} %copy-done) | copy-start | bytes 12582916
  96.5 17.0 %collective-permute-start.2 = (bf16[18,1,128,128]{3,2,1,0:T(8,128)(2,1)S(1)}, bf16[18,1,128,128]{3,2,1,0:T(8,128)(2,1)S(1)}, u32[]{:S(2)}, u32[]{:S(2)}) collective-permute-start(bf16[18,1,128,128]{3,2,1,0:T(8,128)(2,1)S(1)} %copy.36), channel_id=1, source_target_pairs={{1,0},{2,1},{3,2},{4,3},{5,4},{6,5},{7,6},{8,7},{9,8},{10,9},{11,1... | collective-permute-start | bytes 1769480 | tf_op jit(solution)/shard_map/ppermute | solution.py:21
  97.8 16.9 %collective-permute-start.1 = (bf16[18,1,128,128]{3,2,1,0:T(8,128)(2,1)S(1)}, bf16[18,1,128,128]{3,2,1,0:T(8,128)(2,1)S(1)}, u32[]{:S(2)}, u32[]{:S(2)}) collective-permute-start(bf16[18,1,128,128]{3,2,1,0:T(8,128)(2,1)S(1)} %copy.35), channel_id=1, source_target_pairs={{0,1},{1,2},{2,3},{3,4},{4,5},{5,6},{6,7},{7,8},{8,9},{9,10},{10,1... | collective-permute-start | bytes 1769480 | tf_op jit(solution)/shard_map/ppermute | solution.py:18
  113.9 4.2 %copy-start.5 = (bf16[3,3,3,128,128]{4,3,2,1,0:T(8,128)(2,1)S(1)}, bf16[3,3,3,128,128]{4,3,2,1,0:T(8,128)(2,1)}, u32[]{:S(2)}) copy-start(bf16[3,3,3,128,128]{4,3,2,1,0:T(8,128)(2,1)} %param.13) | copy-start | bytes 2654212
  130.5 12.3 %copy-start.2 = (bf16[16,8,128,128]{3,2,1,0:T(8,128)(2,1)S(1)}, bf16[16,8,128,128]{3,2,1,0:T(8,128)(2,1)}, u32[]{:S(2)}) copy-start(bf16[16,8,128,128]{3,2,1,0:T(8,128)(2,1)} %gather_fusion.3) | copy-start | bytes 12582916
  130.5 12.3 %copy-start.7 = (f32[128]{0:T(128)S(1)}, f32[128]{0:T(128)}, u32[]{:S(2)}) copy-start(f32[128]{0:T(128)} %param.12) | copy-start | bytes 1540
where the time goes:
time: 285 us; the launch traced here: 284 us
  blocking collectives  106 us (37%)
  waiting for transfers between devices  62.4 us (22%)
  matrix products  47.7 us (17%)
  local copies, waits for them, and re-layouts  29.2 us (10%)
  other arithmetic  26 us (9%)
  starting transfers between devices  12.9 us (5%)
    all_to_all x1, blocking collectives, local(): lax.all_to_all(encoded, 'space', split_axis=2, concat_axis=1, tiled=True)  106 us
    conv_general_dilated x3, matrix products, spatial_conv(): lax.conv_general_dilated(inputs, kernel, (1, 1), padding, dimension_numbe...  47.7 us
    all_to_all x1, waiting for transfers between devices, local(): lax.all_to_all(packed, 'slab', split_axis=0, concat_axis=0, tiled=True)  42.5 us
    ppermute x1, waiting for transfers between devices, with_halo(): lax.ppermute(lax.slice_in_dim(block, 0, width, axis=dim), axis, backward)  10.8 us
    ppermute x1, waiting for transfers between devices, passed_along(): return lax.ppermute(block, axis, route)  8.38 us
    all_to_all x1, local copies, waits for them, and re-layouts, local(): lax.all_to_all(encoded, 'space', split_axis=2, concat_axis=1, tiled=True)  8.25 us
    convert_element_type x1, other arithmetic, normalize(): jax.nn.silu(values * lax.rsqrt(meansq + 1e-06) * norm_gain)  7.2 us
  transfers between devices with their start and end apart: 4, of which 4 were waited for; matrix products, arithmetic and copies ran while one was open for 2% of the time, Pallas kernels for 0%

commit v1 on v0

--- a/solution.py
+++ b/solution.py
@@ -95,7 +95,12 @@
     padded = with_halo(extended, (("space", 1),), 1)
     branch = causal_branch(padded, masks, conv_weight, conv_bias, ((0, 0), (1, 1)))
     encoded = arranged.astype(jnp.float32) + branch
-    return lax.all_to_all(encoded, "space", split_axis=2, concat_axis=1, tiled=True)
+    return jnp.concatenate(
+        lax.all_to_all(
+            jnp.stack(jnp.split(encoded, lax.axis_size("space"), axis=2)), "space", 0, 0
+        ),
+        axis=1,
+    )
 
 
 def solution(mesh):

time: 285 us -> 278 us (0.975)
  local copies, waits for them, and re-layouts: 29.2 us -> 23.2 us
  matrix products: 47.7 us -> 43 us
  waiting for transfers between devices: 62.4 us -> 65.7 us
    all_to_all x1 -> x0, local copies, waits for them, and re-layouts: 8.25 us -> none  [local(): lax.all_to_all(encoded, 'space', split_axis=2, concat_axis=1, tiled=True)]
    reshape x0 -> x1, local copies, waits for them, and re-layouts: none -> 5.96 us  [local(): jnp.concatenate(lax.all_to_all(jnp.stack(jnp.split(encoded, lax.axis_size...]
    conv_general_dilated x3, matrix products: 47.7 us -> 43 us  [spatial_conv(): lax.conv_general_dilated(inputs, kernel, (1, 1), padding, dimension_numbe...]
    add x1 -> x0, local copies, waits for them, and re-layouts: 4.41 us -> none  [local(): encoded = arranged.astype(jnp.float32) + branch]
    all_to_all x1, waiting for transfers between devices: 42.5 us -> 45.7 us  [local(): lax.all_to_all(packed, 'slab', split_axis=0, concat_axis=0, tiled=True)]
  transfers between devices with their start and end apart: 4 -> 4, of which waited for: 4 -> 4; matrix products, arithmetic and copies ran while one was open for 2% -> 1% of each run, Pallas kernels for 0% -> 0%
where the time goes in v1:
time: 278 us
  blocking collectives  106 us (38%)
  waiting for transfers between devices  65.7 us (24%)
  matrix products  43 us (15%)
  other arithmetic  26.7 us (10%)
  local copies, waits for them, and re-layouts  23.2 us (8%)
  starting transfers between devices  12.9 us (5%)
    all_to_all x1, blocking collectives, local(): lax.all_to_all(jnp.stack(jnp.split(encoded, lax.axis_size('space'), axis=...  106 us
    all_to_all x1, waiting for transfers between devices, local(): lax.all_to_all(packed, 'slab', split_axis=0, concat_axis=0, tiled=True)  45.7 us
    conv_general_dilated x3, matrix products, spatial_conv(): lax.conv_general_dilated(inputs, kernel, (1, 1), padding, dimension_numbe...  43 us
    ppermute x1, waiting for transfers between devices, with_halo(): lax.ppermute(lax.slice_in_dim(block, 0, width, axis=dim), axis, backward)  10.8 us
    ppermute x1, waiting for transfers between devices, passed_along(): return lax.ppermute(block, axis, route)  8.38 us
    convert_element_type x1, other arithmetic, normalize(): jax.nn.silu(values * lax.rsqrt(meansq + 1e-06) * norm_gain)  7.2 us
    reshape x1, local copies, waits for them, and re-layouts, local(): jnp.concatenate(lax.all_to_all(jnp.stack(jnp.split(encoded, lax.axis_size...  5.96 us
  transfers between devices with their start and end apart: 4, of which 4 were waited for; matrix products, arithmetic and copies ran while one was open for 1% of the time, Pallas kernels for 0%

profile of v1, /device:TPU:64, one launch (start us, length us, event | category | flops | bytes accessed | tf_op | source)
XLA Modules:
  0.0 277.8 jit_solution(8943279138111204007)
XLA Ops:
  0.0 0.7 dynamic_slice.3
  0.7 1.2 sort.34
  2.0 3.2 %sort.35 = (s32[128]{0:T(128)}, s32[128]{0:T(128)S(1)}) sort(s32[128]{0:T(128)} %param.9, s32[128]{0:T(128)S(1)} %iota.23), dimensions={0}, to_apply=%region_1.3 | sort | flops 896 | bytes 2048 | tf_op jit(solution)/shard_map/jit(argsort)/sort | solution.py:79
  5.2 0.7 gather_fusion
  5.9 5.3 %gather_fusion.2 = bf16[16,8,128,128]{3,2,1,0:T(8,128)(2,1)} fusion(bf16[16,8,128,128]{3,2,1,0:T(8,128)(2,1)} %param.8, s32[1024]{0:T(1024)S(1)} %get-tuple-element.19), kind=kCustom, calls=%fused_computation.clone | custom fusion | bytes 8388672 | tf_op jit(solution)/shard_map/jit(_take)/gather | solution.py:77
  11.2 4.7 %broadcast_select_fusion = bf16[16,8,128,128]{3,2,1,0:T(8,128)(2,1)} fusion(bf16[16,8,128,128]{3,2,1,0:T(8,128)(2,1)} %gather_fusion.2, pred[16]{0:T(512)(128)(4,1)S(1)} %compare_and_fusion.1), kind=kLoop, calls=%fused_computation.23 | loop fusion | flops 2097152 | bytes 8388624 | tf_op jit(solution)/shard_map/jit(_take)/select_n | solution.py:77
  15.9 5.0 %all-to-all-start = ((bf16[16,8,128,128]{3,2,1,0:T(8,128)(2,1)}), bf16[16,8,128,128]{3,2,1,0:T(8,128)(2,1)}, u32[]{:S(2)}, u32[]{:S(2)}) async-start(bf16[16,8,128,128]{3,2,1,0:T(8,128)(2,1)} %broadcast_select_fusion), calls=%async_computation | async-start | bytes 8388608 | tf_op jit(solution)/shard_map/all_to_all | solution.py:91
  20.9 0.6 gather_fusion.1
  21.5 0.2 convert_reduce_fusion
  21.7 45.7 %all-to-all-done = bf16[16,8,128,128]{3,2,1,0:T(8,128)(2,1)} async-done(((bf16[16,8,128,128]{3,2,1,0:T(8,128)(2,1)}), bf16[16,8,128,128]{3,2,1,0:T(8,128)(2,1)}, u32[]{:S(2)}, u32[]{:S(2)}) %all-to-all-start) | async-done | bytes 4194336 | tf_op jit(solution)/shard_map/all_to_all | solution.py:91
  67.5 5.2 %gather_fusion.3 = bf16[16,8,128,128]{3,2,1,0:T(8,128)(2,1)} fusion(bf16[16,8,128,128]{3,2,1,0:T(8,128)(2,1)} %all-to-all-done, s32[1024]{0:T(1024)S(1)} %pad_clamp_fusion), kind=kCustom, calls=%fused_computation.1.clone | custom fusion | bytes 8388672 | tf_op jit(solution)/shard_map/jit(_take)/gather | solution.py:92
  72.7 4.9 %fusion = f32[16,8,128]{0,2,1:T(8,128)S(1)} fusion(bf16[16,8,128,128]{3,2,1,0:T(8,128)(2,1)} %gather_fusion.3, pred[16]{0:T(512)(128)(4,1)S(1)} %get-tuple-element.10), kind=kLoop, calls=%fused_computation.7 | loop fusion | flops 8372224 | bytes 4259856 | tf_op jit(solution)/shard_map/reduce_sum | solution.py:37
  77.8 0.2 copy.31
  78.0 7.2 %fusion.7 = bf16[16,8,128,128]{3,0,2,1:T(8,128)(2,1)S(1)} fusion(f32[128]{0:T(128)S(1)} %copy-done.4, f32[16,8,128]{0,2,1:T(8,128)S(1)} %copy.31, bf16[16,8,128,128]{3,2,1,0:T(8,128)(2,1)} %gather_fusion.3, pred[16]{0:T(512)(128)(4,1)S(1)} %get-tuple-element.10), kind=kLoop, calls=%fused_computation.14 | loop fusion | flops 18874368 | bytes 8454672 | tf_op jit(solution)/shard_map/convert_element_type | solution.py:38
  85.2 2.0 copy-done
  87.2 0.5 slice.56
  87.8 1.9 collective-permute-start
  89.7 0.2 reduce-window.9
  89.9 8.4 %collective-permute-done = bf16[2,8,128,128]{3,0,2,1:T(2,128)(2,1)S(1)} collective-permute-done((bf16[2,8,128,128]{3,0,2,1:T(2,128)(2,1)S(1)}, bf16[2,8,128,128]{3,0,2,1:T(2,128)(2,1)S(1)}, u32[]{:S(2)}, u32[]{:S(2)}) %collective-permute-start) | collective-permute-done | bytes 524320 | tf_op jit(solution)/shard_map/ppermute | solution.py:10
  98.3 1.9 pad_maximum_fusion.2
  100.4 1.3 collective-permute-start.2
  101.7 4.8 %collective-permute-start.1 = (bf16[18,1,128,128]{3,2,1,0:T(8,128)(2,1)S(1)}, bf16[18,1,128,128]{3,2,1,0:T(8,128)(2,1)S(1)}, u32[]{:S(2)}, u32[]{:S(2)}) collective-permute-start(bf16[18,1,128,128]{3,2,1,0:T(8,128)(2,1)S(1)} %copy.32), channel_id=1, source_target_pairs={{0,1},{1,2},{2,3},{3,4},{4,5},{5,6},{6,7},{7,8},{8,9},{9,10},{10,1... | collective-permute-start | bytes 1769480 | tf_op jit(solution)/shard_map/ppermute | solution.py:18
  106.6 10.8 %collective-permute-done.2 = bf16[18,1,128,128]{3,2,1,0:T(8,128)(2,1)S(1)} collective-permute-done((bf16[18,1,128,128]{3,2,1,0:T(8,128)(2,1)S(1)}, bf16[18,1,128,128]{3,2,1,0:T(8,128)(2,1)S(1)}, u32[]{:S(2)}, u32[]{:S(2)}) %collective-permute-start.2) | collective-permute-done | bytes 589856 | tf_op jit(solution)/shard_map/ppermute | solution.py:21
  117.4 0.4 copy.35
  117.8 0.8 collective-permute-done.1
  118.6 0.4 copy.34
  119.0 3.0 %pad_maximum_fusion = bf16[18,10,128,128]{3,0,2,1:T(8,128)(2,1)S(1)} fusion(bf16[18,1,128,128]{3,0,2,1:T(8,128)(2,1)S(1)} %copy.35, bf16[16,8,128,128]{3,0,2,1:T(8,128)(2,1)S(1)} %copy-done.1, bf16[2,8,128,128]{3,0,2,1:T(2,128)(2,1)S(1)} %collective-permute-done, bf16[18,1,128,128]{3,0,2,1:T(8,128)(2,1)S(1)} %copy.34), kind=kLoop, calls=%fused_computation.15 | loop fusion | flops 23592960 | bytes 11796480 | tf_op jit(solution)/shard_map/concatenate | solution.py:22
  122.1 12.3 %fusion.9 = f32[16,8,128,128]{3,0,2,1:T(8,128)} fusion(bf16[18,10,128,128]{3,0,2,1:T(8,128)(2,1)S(1)} %pad_maximum_fusion, bf16[16]{0:T(256)(128)(2,1)S(1)} %get-tuple-element.17, bf16[3,3,3,128,128]{4,3,2,1,0:T(8,128)(2,1)S(1)} %copy-done.6), kind=kOutput, calls=%fused_computation.19 | convolution fusion | flops 4817158144 | bytes 13926912 | tf_op jit(solution)/shard_map/conv_general_dilated | solution.py:42
  134.4 12.4 %fusion.10 = f32[16,8,128,128]{3,0,2,1:T(8,128)} fusion(bf16[18,10,128,128]{3,0,2,1:T(8,128)(2,1)S(1)} %pad_maximum_fusion, bf16[16]{0:T(256)(128)(2,1)S(1)} %get-tuple-element.18, bf16[3,3,3,128,128]{4,3,2,1,0:T(8,128)(2,1)S(1)} %copy-done.6), kind=kOutput, calls=%fused_computation.21 | convolution fusion | flops 4817158144 | bytes 13926912 | tf_op jit(solution)/shard_map/conv_general_dilated | solution.py:42
  146.8 18.3 %convert_add_fusion = f32[16,8,128,128]{3,0,2,1:T(8,128)S(1)} fusion(f32[16,8,128,128]{3,0,2,1:T(8,128)} %fusion.10, f32[16,8,128,128]{3,0,2,1:T(8,128)} %fusion.9, f32[128]{0:T(128)S(1)} %copy-done.8, bf16[18,10,128,128]{3,0,2,1:T(8,128)(2,1)} %copy-done.3, bf16[16]{0:T(256)(128)(2,1)S(1)} %get-tuple-element.16, ...), kind=kOutput, calls=%fused_computation.4 | convolution fusion | flops 4829741056 | bytes 34899456 | tf_op jit(solution)/shard_map/conv_general_dilated | solution.py:42
  165.9 105.9 %all_to_all.10 = f32[16,16,8,8,128]{4,1,3,2,0:T(8,128)S(1)} all-to-all(f32[16,16,8,8,128]{4,1,3,2,0:T(8,128)S(1)} %fusion.14), channel_id=1, replica_groups=mesh['slab'=8,'space'=16] {'space'}, dimensions={0} | all-to-all | bytes 16777216 | tf_op jit(solution)/shard_map/all_to_all | solution.py:99
  271.9 6.0 %copy.36 = f32[16,128,8,128]{3,2,1,0:T(8,128)} copy(f32[16,128,8,128]{3,0,2,1:T(8,128)S(1)} %bitcast.93) | data formatting | bytes 16777216 | tf_op jit(solution)/shard_map/reshape | solution.py:98
  (54 shorter events, 1.5 us)
Async XLA Ops:
  11.2 9.6 %copy-start.5 = (s32[128]{0:T(128)S(1)}, s32[128]{0:T(128)}, u32[]{:S(2)}) copy-start(s32[128]{0:T(128)} %param.9) | copy-start | bytes 1540
  15.9 51.6 %all-to-all-start = ((bf16[16,8,128,128]{3,2,1,0:T(8,128)(2,1)}), bf16[16,8,128,128]{3,2,1,0:T(8,128)(2,1)}, u32[]{:S(2)}, u32[]{:S(2)}) async-start(bf16[16,8,128,128]{3,2,1,0:T(8,128)(2,1)} %broadcast_select_fusion), calls=%async_computation | async-start | bytes 8388608 | tf_op jit(solution)/shard_map/all_to_all | solution.py:91
  20.8 57.1 %copy-start.4 = (f32[128]{0:T(128)S(1)}, f32[128]{0:T(128)}, u32[]{:S(2)}) copy-start(f32[128]{0:T(128)} %param.11) | copy-start | bytes 1540
  72.7 17.0 %copy-start.7 = (s32[8]{0:T(128)S(1)}, s32[8]{0:T(128)}, u32[]{:S(2)}) copy-start(s32[8]{0:T(128)} %param.10) | copy-start | bytes 100
  85.2 2.0 copy-start
  87.8 10.5 %collective-permute-start = (bf16[2,8,128,128]{3,0,2,1:T(2,128)(2,1)S(1)}, bf16[2,8,128,128]{3,0,2,1:T(2,128)(2,1)S(1)}, u32[]{:S(2)}, u32[]{:S(2)}) collective-permute-start(bf16[2,8,128,128]{3,0,2,1:T(2,128)(2,1)S(1)} %slice.56), channel_id=1, source_target_pairs={{0,16},{16,32},{32,48},{48,64},{64,80},{80,96},{96,112},{1,17},{17... | collective-permute-start | bytes 1572872 | tf_op jit(solution)/shard_map/ppermute | solution.py:10
  89.9 29.1 %copy-start.1 = (bf16[16,8,128,128]{3,0,2,1:T(8,128)(2,1)S(1)}, bf16[16,8,128,128]{3,0,2,1:T(8,128)(2,1)}, u32[]{:S(2)}) copy-start(bf16[16,8,128,128]{3,0,2,1:T(8,128)(2,1)} %copy-done) | copy-start | bytes 12582916
  100.4 17.0 %collective-permute-start.2 = (bf16[18,1,128,128]{3,2,1,0:T(8,128)(2,1)S(1)}, bf16[18,1,128,128]{3,2,1,0:T(8,128)(2,1)S(1)}, u32[]{:S(2)}, u32[]{:S(2)}) collective-permute-start(bf16[18,1,128,128]{3,2,1,0:T(8,128)(2,1)S(1)} %copy.33), channel_id=1, source_target_pairs={{1,0},{2,1},{3,2},{4,3},{5,4},{6,5},{7,6},{8,7},{9,8},{10,9},{11,1... | collective-permute-start | bytes 1769480 | tf_op jit(solution)/shard_map/ppermute | solution.py:21
  101.7 16.9 %collective-permute-start.1 = (bf16[18,1,128,128]{3,2,1,0:T(8,128)(2,1)S(1)}, bf16[18,1,128,128]{3,2,1,0:T(8,128)(2,1)S(1)}, u32[]{:S(2)}, u32[]{:S(2)}) collective-permute-start(bf16[18,1,128,128]{3,2,1,0:T(8,128)(2,1)S(1)} %copy.32), channel_id=1, source_target_pairs={{0,1},{1,2},{2,3},{3,4},{4,5},{5,6},{6,7},{7,8},{8,9},{9,10},{10,1... | collective-permute-start | bytes 1769480 | tf_op jit(solution)/shard_map/ppermute | solution.py:18
  106.5 15.5 %copy-start.6 = (bf16[3,3,3,128,128]{4,3,2,1,0:T(8,128)(2,1)S(1)}, bf16[3,3,3,128,128]{4,3,2,1,0:T(8,128)(2,1)}, u32[]{:S(2)}) copy-start(bf16[3,3,3,128,128]{4,3,2,1,0:T(8,128)(2,1)} %param.13) | copy-start | bytes 2654212
  122.0 12.3 %copy-start.3 = (bf16[18,10,128,128]{3,0,2,1:T(8,128)(2,1)}, bf16[18,10,128,128]{3,0,2,1:T(8,128)(2,1)S(1)}, u32[]{:S(2)}) copy-start(bf16[18,10,128,128]{3,0,2,1:T(8,128)(2,1)S(1)} %pad_maximum_fusion) | copy-start | bytes 17694724
  134.4 12.4 %copy-start.2 = (bf16[16,8,128,128]{3,2,1,0:T(8,128)(2,1)S(1)}, bf16[16,8,128,128]{3,2,1,0:T(8,128)(2,1)}, u32[]{:S(2)}) copy-start(bf16[16,8,128,128]{3,2,1,0:T(8,128)(2,1)} %gather_fusion.3) | copy-start | bytes 12582916
  134.4 12.4 %copy-start.8 = (f32[128]{0:T(128)S(1)}, f32[128]{0:T(128)}, u32[]{:S(2)}) copy-start(f32[128]{0:T(128)} %param.12) | copy-start | bytes 1540
